TPU v7x, 32 devices: a whole 2x2x4 slice. The times are simulated.
32 devices in a mesh: tm: 4 (over y, x), pts: 8 (over z, core).
Axes of the slice: x: 2, y: 2, z: 4, core: 2. Of those that a mesh axis runs over, the one named last changes fastest.
Arguments:
- series: bfloat16 [8192, 3, 8192], P('tm', None, 'pts'), may hold values from -6 to 6
- weights: float32 [8192], P('pts'), may hold values from 1.2207031e-05 to 0.00012207031
- freq_bins: int32 [16], replicated, may hold values from 1 to 255
Outputs:
- cross_gram: float32 [16, 2, 32, 32], P('tm')
- spatial_modes: bfloat16 [16, 2, 32, 3, 8192], P('tm', None, None, None, 'pts')
All inputs are finite; a program needn't handle non-finite values.
Results may differ from a plain program's by a relative error of at most 0.0067.
Values may be sent and summed in bfloat16 or wider, within the bound.
A program may use at most 128 MiB of HBM per device.

v0:
```python
import jax
import jax.numpy as jnp
from jax import lax
from jax.sharding import PartitionSpec as P

NFFT = 512
NB = 32
NF = 16
ITERS = 4


def from_behind(block, axis, distance):
    devices = range(lax.axis_size(axis))
    route = [((i - distance) % len(devices), i) for i in devices]
    return lax.ppermute(block, axis, route)


def build_table(freq_bins):
    sample_index = jnp.arange(NFFT, dtype=jnp.int32)
    window = (
        0.5 - 0.5 * jnp.cos(2.0 * jnp.pi * sample_index.astype(jnp.float32) / NFFT)
    ) * jnp.sqrt(8.0 / (3.0 * NFFT))
    product_index = freq_bins[:, None] * sample_index[None, :] % NFFT
    phase_angle = 2.0 * jnp.pi * product_index.astype(jnp.float32) / NFFT
    kernel_table = jnp.stack(
        [jnp.cos(phase_angle) * window, -jnp.sin(phase_angle) * window], axis=1
    )
    return kernel_table.reshape(2 * NF, NFFT).astype(jnp.bfloat16)


def matmul_high(left, right):
    return jnp.matmul(left, right, precision=lax.Precision.HIGHEST)


def combine(pair_gram):
    real_part = pair_gram[..., :NB, :NB] + pair_gram[..., NB:, NB:]
    imag_part = pair_gram[..., :NB, NB:] - pair_gram[..., NB:, :NB]
    return jnp.stack([real_part, imag_part], axis=-3)


def inverse_root(cross_gram):
    real_part = cross_gram[..., 0, :, :]
    imag_part = cross_gram[..., 1, :, :]
    norm_value = jnp.sqrt(jnp.sum(cross_gram * cross_gram, axis=(-3, -2, -1)))
    upper_rows = jnp.concatenate([real_part, -imag_part], axis=-1)
    lower_rows = jnp.concatenate([imag_part, real_part], axis=-1)
    current = jnp.concatenate([upper_rows, lower_rows], axis=-2) / norm_value[..., None, None]
    identity = jnp.eye(2 * NB, dtype=jnp.float32)
    inv_root = jnp.broadcast_to(identity, current.shape)
    for iteration in range(ITERS):
        factor = 0.5 * (3.0 * identity - matmul_high(inv_root, current))
        current = matmul_high(current, factor)
        inv_root = matmul_high(factor, inv_root)
    return inv_root


def on_device(series, weights, freq_bins):
    kernel_table = build_table(freq_bins)
    half_len = NFFT // 2
    point_cols = series.shape[1] * series.shape[2]
    local_blocks = series.shape[0] // half_len
    halves = series.reshape(local_blocks, half_len, point_cols)
    first_half = jnp.einsum(
        "kn,jnp->kjp", kernel_table[:, :half_len], halves, preferred_element_type=jnp.float32
    )
    received = from_behind(series[:half_len], "tm", -1)
    following = jnp.concatenate([halves[1:], received.reshape(1, half_len, point_cols)], axis=0)
    second_half = jnp.einsum(
        "kn,jnp->kjp", kernel_table[:, half_len:], following, preferred_element_type=jnp.float32
    )
    coefficients = (first_half + second_half).astype(jnp.bfloat16)
    regrouped = lax.all_to_all(
        coefficients.reshape(NF, 2, local_blocks, point_cols),
        "tm",
        split_axis=0,
        concat_axis=2,
        tiled=True,
    )
    local_bins = regrouped.shape[0]
    freq_rows = regrouped.reshape(local_bins, 2 * NB, point_cols)
    row_weight = jnp.tile(weights, 3)
    weighted = freq_rows.astype(jnp.float32) * row_weight
    weighted_high = weighted.astype(jnp.bfloat16)
    weighted_low = (weighted - weighted_high.astype(jnp.float32)).astype(jnp.bfloat16)
    pair_gram = jnp.einsum(
        "fip,fjp->fij", weighted_high, freq_rows, preferred_element_type=jnp.float32
    )
    pair_gram = pair_gram + jnp.einsum(
        "fip,fjp->fij", weighted_low, freq_rows, preferred_element_type=jnp.float32
    )
    cross_gram = combine(lax.psum(pair_gram, "pts"))
    inv_root = inverse_root(cross_gram).astype(jnp.bfloat16)
    spatial_modes = jnp.einsum(
        "fij,fjp->fip", inv_root, freq_rows, preferred_element_type=jnp.float32
    ).astype(jnp.bfloat16)
    return (cross_gram, spatial_modes.reshape(local_bins, 2, NB, 3, series.shape[2]))


def solution(mesh):
    in_specs = (P("tm", None, "pts"), P("pts"), P())
    out_specs = (P("tm", None, None, None), P("tm", None, None, None, "pts"))
    return jax.shard_map(
        on_device, mesh=mesh, in_specs=in_specs, out_specs=out_specs, check_vma=False
    )
```

profile of v0, /device:TPU:1, one launch (start us, length us, event | category | flops | bytes accessed | tf_op | source)
XLA Modules:
  0.0 244.7 jit_solution(15785877224248194130)
XLA Ops:
  7.2 0.0 slice-start
  7.2 1.4 slice-done
  8.6 1.6 copy.54
  10.1 3.0 %collective-permute-start = (bf16[256,3,1024]{0,2,1:T(8,128)(2,1)}, bf16[256,3,1024]{0,2,1:T(8,128)(2,1)}, u32[]{:S(2)}, u32[]{:S(2)}) collective-permute-start(bf16[256,3,1024]{0,2,1:T(8,128)(2,1)} %copy.54), channel_id=1, source_target_pairs={{8,0},{16,8},{24,16},{0,24},{9,1},{17,9},{25,17},{1,25},{10,2},{18... | collective-permute-start | bytes 4718600 | tf_op jit(solution)/shard_map/ppermute | solution.py:15
  13.1 18.8 %copy.50 = bf16[2048,3,1024]{2,1,0:T(4,128)(2,1)} copy(bf16[2048,3,1024]{2,0,1:T(8,128)(2,1)} %param.3) | data formatting | bytes 25165824 | tf_op jit(solution)/shard_map/reshape | solution.py:62
  32.0 0.0 copy-start.1
  32.0 10.2 %slice.29 = bf16[1792,3,1024]{2,0,1:T(8,128)(2,1)} slice(bf16[2048,3,1024]{2,0,1:T(8,128)(2,1)} %param.3), slice={[256:2048], [0:3], [0:1024]} | slice | bytes 22020096 | tf_op jit(solution)/shard_map/slice | solution.py:67
  42.2 0.0 copy-done.1
  42.2 0.2 multiply_convert_fusion.1
  42.5 34.5 %reshape.188 = bf16[8,256,3072]{2,1,0:T(8,128)(2,1)} reshape(bf16[2048,3,1024]{2,1,0:T(4,128)(2,1)} %copy.50) | data formatting | bytes 25165824 | tf_op jit(solution)/shard_map/reshape | solution.py:62
  77.0 16.8 %copy.51 = bf16[1792,3,1024]{2,1,0:T(4,128)(2,1)} copy(bf16[1792,3,1024]{2,0,1:T(8,128)(2,1)} %slice.29) | data formatting | bytes 22020096 | tf_op jit(solution)/shard_map/slice | solution.py:67
  93.8 30.2 %reshape.189 = bf16[7,256,3072]{2,1,0:T(8,128)(2,1)} reshape(bf16[1792,3,1024]{2,1,0:T(4,128)(2,1)} %copy.51) | data formatting | bytes 22020096 | tf_op jit(solution)/shard_map/slice | solution.py:67
  124.0 6.8 %fusion.32 = f32[32,8,3072]{2,0,1:T(8,128)S(1)} fusion(bf16[8,256,3072]{2,1,0:T(8,128)(2,1)} %reshape.188, bf16[32,512]{1,0:T(8,128)(2,1)S(1)} %convert_element_type.55), kind=kOutput, calls=%fused_computation.49 | convolution fusion | flops 402653184 | bytes 15745024 | tf_op jit(solution)/shard_map/kn,jnp->kjp/dot_general | solution.py:63
  130.8 0.0 collective-permute-done
  130.8 2.6 %copy.45 = bf16[1,256,3072]{2,1,0:T(8,128)(2,1)} copy(bf16[1,256,3072]{1,2,0:T(8,128)(2,1)} %bitcast.2) | data formatting | bytes 3145728 | tf_op jit(solution)/shard_map/reshape | solution.py:67
  133.4 7.0 %fusion.7 = bf16[32,8,3072]{2,0,1:T(8,128)(2,1)} fusion(f32[32,8,3072]{2,0,1:T(8,128)S(1)} %fusion.32, bf16[1,256,3072]{2,1,0:T(8,128)(2,1)} %copy.45, bf16[7,256,3072]{2,1,0:T(8,128)(2,1)} %reshape.189, bf16[32,512]{1,0:T(8,128)(2,1)S(1)} %convert_element_type.55), kind=kOutput, calls=%fused_computation.5 | convolution fusion | flops 429391872 | bytes 17317888 | tf_op jit(solution)/shard_map/kn,jnp->kjp/dot_general | solution.py:68
  140.4 3.5 %reshape.183 = bf16[16,2,8,3072]{3,1,0,2:T(2,128)(2,1)S(1)} reshape(bf16[32,8,3072]{2,0,1:T(8,128)(2,1)} %fusion.7) | data formatting | bytes 3145728 | tf_op jit(solution)/shard_map/reshape | solution.py:73
  143.9 0.0 copy-start
  144.0 2.7 %copy.46 = bf16[16,2,8,3072]{3,1,2,0:T(2,128)(2,1)} copy(bf16[16,2,8,3072]{3,1,0,2:T(2,128)(2,1)S(1)} %reshape.183) | data formatting | bytes 3145728 | tf_op jit(solution)/shard_map/reshape | solution.py:73
  146.6 3.6 %all-to-all-start = ((bf16[16,2,8,3072]{3,1,2,0:T(2,128)(2,1)}), bf16[16,2,8,3072]{3,1,2,0:T(2,128)(2,1)S(1)}, u32[]{:S(2)}, u32[]{:S(2)}) async-start(bf16[16,2,8,3072]{3,1,2,0:T(2,128)(2,1)} %copy.46), calls=%async_computation | async-start | bytes 3145728 | tf_op jit(solution)/shard_map/all_to_all | solution.py:72
  150.2 0.2 all-reduce.2.cloned.1.call-start
  150.4 0.0 copy-done
  150.5 18.4 %all-to-all-done = bf16[16,2,8,3072]{3,1,2,0:T(2,128)(2,1)S(1)} async-done(((bf16[16,2,8,3072]{3,1,2,0:T(2,128)(2,1)}), bf16[16,2,8,3072]{3,1,2,0:T(2,128)(2,1)S(1)}, u32[]{:S(2)}, u32[]{:S(2)}) %all-to-all-start) | async-done | bytes 1572896 | tf_op jit(solution)/shard_map/all_to_all | solution.py:72
  168.9 0.3 copy.47
  169.2 0.6 fusion.11
  169.8 1.3 fusion.16
  171.1 0.0 all-reduce.2.cloned.1.call-update
  171.1 53.8 %all-reduce.2.cloned.1.call-done = f32[4,64,64]{2,1,0:T(8,128)} async-done(((f32[4,64,64]{2,1,0:T(8,128)}), f32[4,64,64]{2,1,0:T(8,128)}) %all-reduce.2.cloned.1.call-update) | async-done | bytes 65552 | tf_op jit(solution)/shard_map/psum | solution.py:91
  224.9 1.0 fusion.35
  226.0 0.1 multiply_reduce_fusion
  226.1 0.4 fusion.20
  226.5 0.3 fusion.34
  226.8 0.2 fusion.21
  227.0 0.3 fusion.19
  227.3 0.3 fusion.37
  227.6 0.3 fusion.36
  227.8 0.3 fusion.18
  228.1 0.3 fusion.39
  228.4 0.3 fusion.38
  228.6 0.3 fusion.17
  228.9 0.3 convolution_convert_fusion.1
  229.2 1.7 convolution_convert_fusion
  230.8 4.6 %reshape.185 = bf16[4,2,32,3,1024]{4,3,2,1,0:T(4,128)(2,1)S(1)} reshape(bf16[4,64,3072]{2,1,0:T(8,128)(2,1)} %convolution_convert_fusion) | data formatting | bytes 3145728 | tf_op jit(solution)/shard_map/reshape | solution.py:96
  235.4 1.8 copy.49
  237.2 0.7 copy.48
  (9 shorter events, 0.1 us)
Async XLA Ops:
  7.2 1.4 slice-start
  10.1 120.7 %collective-permute-start = (bf16[256,3,1024]{0,2,1:T(8,128)(2,1)}, bf16[256,3,1024]{0,2,1:T(8,128)(2,1)}, u32[]{:S(2)}, u32[]{:S(2)}) collective-permute-start(bf16[256,3,1024]{0,2,1:T(8,128)(2,1)} %copy.54), channel_id=1, source_target_pairs={{8,0},{16,8},{24,16},{0,24},{9,1},{17,9},{25,17},{1,25},{10,2},{18... | collective-permute-start | bytes 4718600 | tf_op jit(solution)/shard_map/ppermute | solution.py:15
  32.0 10.3 %copy-start.1 = (s32[16]{0:T(128)S(1)}, s32[16]{0:T(128)}, u32[]{:S(2)}) copy-start(s32[16]{0:T(128)} %param.5) | copy-start | bytes 196
  143.9 6.5 %copy-start = (f32[1024]{0:T(1024)S(1)}, f32[1024]{0:T(1024)}, u32[]{:S(2)}) copy-start(f32[1024]{0:T(1024)} %param.4) | copy-start | bytes 12292
  146.6 22.2 %all-to-all-start = ((bf16[16,2,8,3072]{3,1,2,0:T(2,128)(2,1)}), bf16[16,2,8,3072]{3,1,2,0:T(2,128)(2,1)S(1)}, u32[]{:S(2)}, u32[]{:S(2)}) async-start(bf16[16,2,8,3072]{3,1,2,0:T(2,128)(2,1)} %copy.46), calls=%async_computation | async-start | bytes 3145728 | tf_op jit(solution)/shard_map/all_to_all | solution.py:72
  150.2 74.7 %all-reduce.2.cloned.1.call-start = ((), (), s32[]{:S(2)}) async-start(), calls=%async_computation.1 | async-start | bytes 262144 | tf_op jit(solution)/shard_map/psum | solution.py:91
Sparse Core Ops, SparseCore 0:
  171.2 53.6 all-reduce.1
where the time goes:
time: 249 us; the launch traced here: 245 us
  local copies, waits for them, and re-layouts  130 us (52%)
  waiting for transfers between devices  72.2 us (29%)
  matrix products  20.3 us (8%)
  between operations  14.3 us (6%)
  starting transfers between devices  6.78 us (3%)
    slice x3, local copies, waits for them, and re-layouts, on_device(): halves[1:]  57.2 us
    psum x1, waiting for transfers between devices, on_device(): cross_gram = combine(lax.psum(pair_gram, 'pts'))  53.8 us
    reshape x2, local copies, waits for them, and re-layouts, on_device(): halves = series.reshape(local_blocks, half_len, point_cols)  53.3 us
    all_to_all x1, waiting for transfers between devices, on_device(): lax.all_to_all(coefficients.reshape(NF, 2, local_blocks, point_cols), 'tm...  18.4 us
    dot_general x1, matrix products, on_device(): jnp.einsum('kn,jnp->kjp', kernel_table[:, half_len:], following, preferre...  7.03 us
    dot_general x1, matrix products, on_device(): jnp.einsum('kn,jnp->kjp', kernel_table[:, :half_len], halves, preferred_e...  6.84 us
    reshape x2, local copies, waits for them, and re-layouts, on_device(): coefficients.reshape(NF, 2, local_blocks, point_cols)  6.16 us
  transfers between devices with their start and end apart: 3, of which 2 were waited for; matrix products, arithmetic and copies ran while one was open for 48% of the time, Pallas kernels for 0%

commit v1 on v0

v1 whole, which is shorter than its diff:
```python
import functools

import jax
import jax.numpy as jnp
from jax import lax
from jax.experimental import pallas as pl
from jax.experimental.pallas import tpu as pltpu
from jax.sharding import PartitionSpec as P

NFFT = 512
NB = 32
NF = 16
ITERS = 4
HALF = NFFT // 2
CHUNK = 256
MESH = pl.DeviceIdType.MESH
F32 = jnp.float32
BF16 = jnp.bfloat16


def build_table(freq_bins):
    sample_index = jnp.arange(NFFT, dtype=jnp.int32)
    window = (
        0.5 - 0.5 * jnp.cos(2.0 * jnp.pi * sample_index.astype(jnp.float32) / NFFT)
    ) * jnp.sqrt(8.0 / (3.0 * NFFT))
    product_index = freq_bins[:, None] * sample_index[None, :] % NFFT
    phase_angle = 2.0 * jnp.pi * product_index.astype(jnp.float32) / NFFT
    kernel_table = jnp.stack(
        [jnp.cos(phase_angle) * window, -jnp.sin(phase_angle) * window], axis=1
    )
    return kernel_table.reshape(2 * NF, NFFT).astype(jnp.bfloat16)


def dot_high(left, right):
    return jnp.dot(
        left, right, precision=lax.Precision.HIGHEST, preferred_element_type=F32
    )


def dot_t(left, right, **kw):
    return lax.dot_general(
        left, right, (((1,), (1,)), ((), ())), preferred_element_type=F32, **kw
    )


def eye(size):
    row = lax.broadcasted_iota(jnp.int32, (size, size), 0)
    col = lax.broadcasted_iota(jnp.int32, (size, size), 1)
    return (row == col).astype(F32)


def gather_order(rows, lb, lf):
    new = lax.broadcasted_iota(jnp.int32, (rows, rows), 0)
    old = lax.broadcasted_iota(jnp.int32, (rows, rows), 1)
    per = 2 * lf
    old_new = (old % per) * NB + old // per
    return (new == old_new).astype(F32)


def inverse_root(real, imag):
    norm = jnp.sqrt(
        jnp.sum(real * real + imag * imag, axis=(0, 1), keepdims=True)
    )
    upper = jnp.concatenate([real, -imag], axis=1)
    lower = jnp.concatenate([imag, real], axis=1)
    y = jnp.concatenate([upper, lower], axis=0) / norm
    ident = eye(2 * NB)
    z = None
    for it in range(ITERS):
        zy = y if z is None else dot_high(z, y)
        s = 0.5 * (3.0 * ident - zy)
        if it < ITERS - 1:
            y = dot_high(y, s)
        z = s if z is None else dot_high(s, z)
    return z


def kernel(nt, ns, series, table_ref, w_ref, cross_ref, modes_ref,
           xbuf, send, land, xall, grams, in_sem, a2a_send, a2a_recv,
           ar_send, ar_recv):
    t = lax.axis_index("tm")
    s = lax.axis_index("pts")
    nq = xbuf.shape[0]
    lb = NB // nt
    lf = NF // nt
    per = 2 * lf
    part = lb * per
    rows = nt * part
    for q in range(nq):
        pltpu.make_async_copy(
            series.at[:, :, pl.ds(q * CHUNK, CHUNK)], xbuf.at[q], in_sem.at[q]
        ).start()
    barrier = pltpu.get_barrier_semaphore()
    for k in range(1, nt):
        pl.semaphore_signal(barrier, inc=1, device_id={"tm": lax.rem(t + k, nt)},
                            device_id_type=MESH)
    for k in range(1, ns):
        pl.semaphore_signal(barrier, inc=1, device_id={"pts": lax.rem(s + k, ns)},
                            device_id_type=MESH)
    pl.semaphore_wait(barrier, nt + ns - 2)

    def peer_copy(q, k):
        to = lax.rem(t + k, nt)
        return pltpu.make_async_remote_copy(
            src_ref=send.at[q, to], dst_ref=land.at[q, k],
            send_sem=a2a_send.at[q, k], recv_sem=a2a_recv.at[q, k],
            device_id={"tm": to}, device_id_type=MESH,
        )

    gram = jnp.zeros((rows, rows), F32)

    def consume(q, gram):
        cols = pl.ds(q * CHUNK, CHUNK)
        for k in range(1, nt):
            peer_copy(q, k).wait_recv()
        weight = w_ref[:, q * CHUNK:(q + 1) * CHUNK]
        for c in range(3):
            for src in range(nt):
                at = lax.rem(t - src + nt, nt)
                nxt = lax.rem(t - src - 1 + nt, nt)
                main = part - 2 * per
                xall[c, src * part:src * part + main, cols] = land[q, at, c, :main, :]
                tail = land[q, at, c, main:part, :].astype(F32)
                halo = land[q, nxt, c, part:part + 2 * per, :].astype(F32)
                fixed = tail[per:] + (halo[:per] + halo[per:])
                xall[c, src * part + main:(src + 1) * part, cols] = jnp.concatenate(
                    [tail[:per], fixed], axis=0).astype(BF16)
            x = xall[c, :, cols]
            xw = x.astype(F32) * weight
            hi = xw.astype(BF16)
            lo = (xw - hi.astype(F32)).astype(BF16)
            gram = gram + dot_t(hi, x) + dot_t(lo, x)
        return gram

    for q in range(nq):
        pltpu.make_async_copy(
            series.at[:, :, pl.ds(q * CHUNK, CHUNK)], xbuf.at[q], in_sem.at[q]
        ).wait()
        for c in range(3):
            firsts, seconds = [], []
            for j in range(lb):
                block = xbuf[q, c, j * HALF:(j + 1) * HALF, :]
                both = jnp.dot(table_ref[...], block, preferred_element_type=F32)
                firsts.append(both[:2 * NF])
                seconds.append(both[2 * NF:])
            sums = [firsts[j] + seconds[j + 1] for j in range(lb - 1)]
            sums.append(firsts[lb - 1])
            halo_hi = seconds[0].astype(BF16).astype(F32)
            sums += [halo_hi, seconds[0] - halo_hi]
            for d in range(nt):
                send[q, d, c] = jnp.concatenate(
                    [v[d * per:(d + 1) * per] for v in sums], axis=0
                ).astype(BF16)
        for k in range(1, nt):
            peer_copy(q, k).start()
        land[q, 0] = send[q, t]
        if q > 0:
            gram = consume(q - 1, gram)
    gram = consume(nq - 1, gram)

    order = gather_order(rows, lb, lf)
    gram = dot_t(dot_high(order, gram), order, precision=lax.Precision.HIGHEST)
    for f in range(lf):
        a = f * 2 * NB
        b = a + NB
        e = b + NB
        grams[0, f, 0] = gram[a:b, a:b] + gram[b:e, b:e]
        grams[0, f, 1] = gram[a:b, b:e] - gram[b:e, a:b]

    def gram_copy(k):
        return pltpu.make_async_remote_copy(
            src_ref=grams.at[0], dst_ref=grams.at[k],
            send_sem=ar_send.at[k], recv_sem=ar_recv.at[k],
            device_id={"pts": lax.rem(s + k, ns)}, device_id_type=MESH,
        )

    for k in range(1, ns):
        gram_copy(k).start()
    for k in range(1, ns):
        gram_copy(k).wait_recv()
    total = grams[lax.rem(s, ns)]
    for k in range(1, ns):
        total = total + grams[lax.rem(s - k + ns, ns)]
    cross_ref[...] = total
    roots = []
    for f in range(lf):
        z = inverse_root(total[f, 0], total[f, 1]).astype(BF16).astype(F32)
        pieces = []
        if f:
            pieces.append(jnp.zeros((2 * NB, f * 2 * NB), F32))
        pieces.append(z)
        if f < lf - 1:
            pieces.append(jnp.zeros((2 * NB, (lf - 1 - f) * 2 * NB), F32))
        roots.append(jnp.concatenate(pieces, axis=1))
    mix = jnp.concatenate(roots, axis=0).astype(BF16)
    mix = jnp.dot(mix, order.astype(BF16), preferred_element_type=F32).astype(BF16)
    for c in range(3):
        for q in range(nq):
            cols = pl.ds(q * CHUNK, CHUNK)
            out = jnp.dot(mix, xall[c, :, cols], preferred_element_type=F32)
            modes_ref[:, :, c, :, cols] = out.astype(BF16).reshape(lf, 2, NB, CHUNK)
    for q in range(nq):
        for k in range(1, nt):
            peer_copy(q, k).wait_send()
    for k in range(1, ns):
        gram_copy(k).wait_send()


def on_device(nt, ns, series, weights, freq_bins):
    table = build_table(freq_bins)
    table = jnp.concatenate([table[:, :HALF], table[:, HALF:]], axis=0)
    points = series.shape[2]
    nq = points // CHUNK
    lb, lf = NB // nt, NF // nt
    rows = NB * 2 * lf
    part = lb * 2 * lf
    vmem = pl.BlockSpec(memory_space=pltpu.VMEM)
    cross, modes = pl.pallas_call(
        functools.partial(kernel, nt, ns),
        out_shape=(
            jax.ShapeDtypeStruct((lf, 2, NB, NB), F32),
            jax.ShapeDtypeStruct((lf, 2, 3, NB, points), BF16),
        ),
        in_specs=[pl.BlockSpec(memory_space=pl.ANY), vmem, vmem],
        out_specs=(vmem, vmem),
        scratch_shapes=[
            pltpu.VMEM((nq, 3, series.shape[0], CHUNK), BF16),
            pltpu.VMEM((nq, nt, 3, part + 4 * lf, CHUNK), BF16),
            pltpu.VMEM((nq, nt, 3, part + 4 * lf, CHUNK), BF16),
            pltpu.VMEM((3, rows, points), BF16),
            pltpu.VMEM((ns, lf, 2, NB, NB), F32),
            pltpu.SemaphoreType.DMA((nq,)),
            pltpu.SemaphoreType.DMA((nq, nt)),
            pltpu.SemaphoreType.DMA((nq, nt)),
            pltpu.SemaphoreType.DMA((ns,)),
            pltpu.SemaphoreType.DMA((ns,)),
        ],
        compiler_params=pltpu.CompilerParams(
            collective_id=0, has_side_effects=True, vmem_limit_bytes=56 * 2**20
        ),
    )(series.transpose(1, 0, 2), table, weights.reshape(1, points))
    return cross, modes.transpose(0, 1, 3, 2, 4)


def solution(mesh):
    nt, ns = mesh.shape["tm"], mesh.shape["pts"]
    in_specs = (P("tm", None, "pts"), P("pts"), P())
    out_specs = (P("tm", None, None, None), P("tm", None, None, None, "pts"))
    return jax.shard_map(
        functools.partial(on_device, nt, ns), mesh=mesh, in_specs=in_specs,
        out_specs=out_specs, check_vma=False
    )
```

time: 249 us -> 66.2 us (0.27)
  the two profiles are of different devices: /device:TPU:1 before, /device:TPU:25 now
where the time goes in v1:
time: 66.2 us; the launch traced here: 65.9 us
  Pallas kernels  59.3 us (90%)
  local copies, waits for them, and re-layouts  4.37 us (7%)
  other arithmetic  1.54 us (2%)
  between operations  0.67 us (1%)
    pallas_call x1, Pallas kernels, on_device(): pl.pallas_call(functools.partial(kernel, nt, ns), out_shape=(jax.ShapeDty...  59.3 us
    unnamed x2, local copies, waits for them, and re-layouts  4.31 us

profile of v1, /device:TPU:25, one launch (start us, length us, event | category | flops | bytes accessed | tf_op | source)
XLA Modules:
  0.0 65.9 jit_solution(10741807925675566775)
XLA Ops:
  0.7 0.9 %multiply_convert_fusion.1 = (bf16[16,1,512]{2,0,1:T(8,128)(2,1)S(1)}, bf16[16,1,512]{2,0,1:T(8,128)(2,1)S(1)}) fusion(f32[512]{0:T(512)S(1)} %subtract_multiply_fusion, s32[16]{0:T(128)} %param.5), kind=kLoop, calls=%fused_computation.9 | loop fusion | flops 155648 | bytes 34880 | tf_op jit(solution)/shard_map/convert
  1.6 0.6 pad_maximum_fusion.1.table_ref
  2.3 59.3 %shard_map.50 = (f32[4,2,32,32]{3,2,1,0:T(8,128)}, bf16[4,2,3,32,1024]{4,3,2,1,0:T(8,128)(2,1)}) custom-call(bf16[3,2048,1024]{2,1,0:T(8,128)(2,1)} %bitcast.3, bf16[64,256]{1,0:T(8,128)(2,1)} %pad_maximum_fusion.1.table_ref, f32[1,1024]{1,0:T(1,128)} %bitcast.5), custom_call_target="tpu_custom_call" | custom-call | tf_op jit(solution)/shard_map/pallas_call | solution.py:218
  61.6 1.6 %copy.8 = f32[4,2,32,32]{3,2,1,0:T(8,128)} copy(f32[4,2,32,32]{3,2,1,0:T(8,128)} %get-tuple-element.12) | data formatting | bytes 65536
  63.2 2.7 %copy.9 = bf16[4,2,32,3,1024]{4,2,3,1,0:T(8,128)(2,1)} copy(bf16[4,2,32,3,1024]{4,2,3,1,0:T(8,128)(2,1)} %bitcast.4) | data formatting | bytes 3145728
  (5 shorter events, 0.1 us)

commit v2 on v1

--- a/solution.py
+++ b/solution.py
@@ -76,8 +76,8 @@
 
 
 def kernel(nt, ns, series, table_ref, w_ref, cross_ref, modes_ref,
-           xbuf, send, land, xall, grams, in_sem, a2a_send, a2a_recv,
-           ar_send, ar_recv):
+           xbuf, send, land, xall, pair, ring, in_sem, a2a_send, a2a_recv,
+           core_send, core_recv, ar_send, ar_recv):
     t = lax.axis_index("tm")
     s = lax.axis_index("pts")
     nq = xbuf.shape[0]
@@ -94,10 +94,14 @@
     for k in range(1, nt):
         pl.semaphore_signal(barrier, inc=1, device_id={"tm": lax.rem(t + k, nt)},
                             device_id_type=MESH)
-    for k in range(1, ns):
-        pl.semaphore_signal(barrier, inc=1, device_id={"pts": lax.rem(s + k, ns)},
+    other = s + 1 - 2 * lax.rem(s, 2)
+    nz = ns // 2
+    pl.semaphore_signal(barrier, inc=1, device_id={"pts": other}, device_id_type=MESH)
+    for k in range(1, nz):
+        pl.semaphore_signal(barrier, inc=1,
+                            device_id={"pts": lax.rem(s + 2 * k, ns)},
                             device_id_type=MESH)
-    pl.semaphore_wait(barrier, nt + ns - 2)
+    pl.semaphore_wait(barrier, nt - 1 + nz)
 
     def peer_copy(q, k):
         to = lax.rem(t + k, nt)
@@ -114,15 +118,17 @@
         for k in range(1, nt):
             peer_copy(q, k).wait_recv()
         weight = w_ref[:, q * CHUNK:(q + 1) * CHUNK]
+        halos = [
+            land[q, lax.rem(t - src - 1 + nt, nt), 3 * part:, :].astype(F32)
+            for src in range(nt)
+        ]
         for c in range(3):
             for src in range(nt):
                 at = lax.rem(t - src + nt, nt)
-                nxt = lax.rem(t - src - 1 + nt, nt)
                 main = part - 2 * per
-                xall[c, src * part:src * part + main, cols] = land[q, at, c, :main, :]
-                tail = land[q, at, c, main:part, :].astype(F32)
-                halo = land[q, nxt, c, part:part + 2 * per, :].astype(F32)
-                fixed = tail[per:] + (halo[:per] + halo[per:])
+                xall[c, src * part:src * part + main, cols] = land[q, at, c * part:c * part + main, :]
+                tail = land[q, at, c * part + main:(c + 1) * part, :].astype(F32)
+                fixed = tail[per:] + halos[src][c * per:(c + 1) * per]
                 xall[c, src * part + main:(src + 1) * part, cols] = jnp.concatenate(
                     [tail[:per], fixed], axis=0).astype(BF16)
             x = xall[c, :, cols]
@@ -136,6 +142,7 @@
         pltpu.make_async_copy(
             series.at[:, :, pl.ds(q * CHUNK, CHUNK)], xbuf.at[q], in_sem.at[q]
         ).wait()
+        edges = []
         for c in range(3):
             firsts, seconds = [], []
             for j in range(lb):
@@ -145,12 +152,16 @@
                 seconds.append(both[2 * NF:])
             sums = [firsts[j] + seconds[j + 1] for j in range(lb - 1)]
             sums.append(firsts[lb - 1])
-            halo_hi = seconds[0].astype(BF16).astype(F32)
-            sums += [halo_hi, seconds[0] - halo_hi]
+            edges.append(seconds[0])
             for d in range(nt):
-                send[q, d, c] = jnp.concatenate(
+                send[q, d, c * part:(c + 1) * part, :] = jnp.concatenate(
                     [v[d * per:(d + 1) * per] for v in sums], axis=0
                 ).astype(BF16)
+        edges.append(jnp.zeros((2 * NF, CHUNK), F32))
+        for d in range(nt):
+            send[q, d, 3 * part:, :] = jnp.concatenate(
+                [v[d * per:(d + 1) * per] for v in edges], axis=0
+            ).astype(BF16)
         for k in range(1, nt):
             peer_copy(q, k).start()
         land[q, 0] = send[q, t]
@@ -160,31 +171,45 @@
 
     order = gather_order(rows, lb, lf)
     gram = dot_t(dot_high(order, gram), order, precision=lax.Precision.HIGHEST)
+    parts = []
     for f in range(lf):
         a = f * 2 * NB
         b = a + NB
         e = b + NB
-        grams[0, f, 0] = gram[a:b, a:b] + gram[b:e, b:e]
-        grams[0, f, 1] = gram[a:b, b:e] - gram[b:e, a:b]
+        parts.append(gram[a:b, a:b] + gram[b:e, b:e])
+        parts.append(gram[a:b, b:e] - gram[b:e, a:b])
+    pair[0] = jnp.concatenate(parts, axis=1)
+
+    core_copy = pltpu.make_async_remote_copy(
+        src_ref=pair.at[0], dst_ref=pair.at[1], send_sem=core_send,
+        recv_sem=core_recv, device_id={"pts": other}, device_id_type=MESH,
+    )
+    core_copy.start()
+    core_copy.wait_recv()
+    ring[0] = pair[0] + pair[1]
 
     def gram_copy(k):
         return pltpu.make_async_remote_copy(
-            src_ref=grams.at[0], dst_ref=grams.at[k],
+            src_ref=ring.at[0], dst_ref=ring.at[k],
             send_sem=ar_send.at[k], recv_sem=ar_recv.at[k],
-            device_id={"pts": lax.rem(s + k, ns)}, device_id_type=MESH,
+            device_id={"pts": lax.rem(s + 2 * k, ns)}, device_id_type=MESH,
         )
 
-    for k in range(1, ns):
+    for k in range(1, nz):
         gram_copy(k).start()
-    for k in range(1, ns):
+    for k in range(1, nz):
         gram_copy(k).wait_recv()
-    total = grams[lax.rem(s, ns)]
-    for k in range(1, ns):
-        total = total + grams[lax.rem(s - k + ns, ns)]
-    cross_ref[...] = total
+    chip = s // 2
+    total = ring[chip]
+    for k in range(1, nz):
+        total = total + ring[lax.rem(chip - k + nz, nz)]
+    total = [total[:, k * NB:(k + 1) * NB] for k in range(2 * lf)]
+    for f in range(lf):
+        cross_ref[f, 0] = total[2 * f]
+        cross_ref[f, 1] = total[2 * f + 1]
     roots = []
     for f in range(lf):
-        z = inverse_root(total[f, 0], total[f, 1]).astype(BF16).astype(F32)
+        z = inverse_root(total[2 * f], total[2 * f + 1]).astype(BF16).astype(F32)
         pieces = []
         if f:
             pieces.append(jnp.zeros((2 * NB, f * 2 * NB), F32))
@@ -202,7 +227,8 @@
     for q in range(nq):
         for k in range(1, nt):
             peer_copy(q, k).wait_send()
-    for k in range(1, ns):
+    core_copy.wait_send()
+    for k in range(1, nz):
         gram_copy(k).wait_send()
 
 
@@ -225,15 +251,18 @@
         out_specs=(vmem, vmem),
         scratch_shapes=[
             pltpu.VMEM((nq, 3, series.shape[0], CHUNK), BF16),
-            pltpu.VMEM((nq, nt, 3, part + 4 * lf, CHUNK), BF16),
-            pltpu.VMEM((nq, nt, 3, part + 4 * lf, CHUNK), BF16),
+            pltpu.VMEM((nq, nt, 3 * part + 8 * lf, CHUNK), BF16),
+            pltpu.VMEM((nq, nt, 3 * part + 8 * lf, CHUNK), BF16),
             pltpu.VMEM((3, rows, points), BF16),
-            pltpu.VMEM((ns, lf, 2, NB, NB), F32),
+            pltpu.VMEM((2, NB, 2 * lf * NB), F32),
+            pltpu.VMEM((ns // 2, NB, 2 * lf * NB), F32),
             pltpu.SemaphoreType.DMA((nq,)),
             pltpu.SemaphoreType.DMA((nq, nt)),
             pltpu.SemaphoreType.DMA((nq, nt)),
-            pltpu.SemaphoreType.DMA((ns,)),
-            pltpu.SemaphoreType.DMA((ns,)),
+            pltpu.SemaphoreType.DMA,
+            pltpu.SemaphoreType.DMA,
+            pltpu.SemaphoreType.DMA((ns // 2,)),
+            pltpu.SemaphoreType.DMA((ns // 2,)),
         ],
         compiler_params=pltpu.CompilerParams(
             collective_id=0, has_side_effects=True, vmem_limit_bytes=56 * 2**20

time: 66.2 us -> 47.4 us (0.72)
  the two profiles are of different devices: /device:TPU:25 before, /device:TPU:1 now
where the time goes in v2:
time: 47.4 us; the launch traced here: 47.2 us
  Pallas kernels  40.6 us (86%)
  local copies, waits for them, and re-layouts  4.37 us (9%)
  other arithmetic  1.54 us (3%)
  between operations  0.67 us (1%)
    pallas_call x1, Pallas kernels, on_device(): pl.pallas_call(functools.partial(kernel, nt, ns), out_shape=(jax.ShapeDty...  40.6 us
    unnamed x2, local copies, waits for them, and re-layouts  4.31 us

profile of v2, /device:TPU:1, one launch (start us, length us, event | category | flops | bytes accessed | tf_op | source)
XLA Modules:
  0.0 47.2 jit_solution(10158999759494969871)
XLA Ops:
  0.7 0.9 %multiply_convert_fusion.1 = (bf16[16,1,512]{2,0,1:T(8,128)(2,1)S(1)}, bf16[16,1,512]{2,0,1:T(8,128)(2,1)S(1)}) fusion(f32[512]{0:T(512)S(1)} %subtract_multiply_fusion, s32[16]{0:T(128)} %param.5), kind=kLoop, calls=%fused_computation.9 | loop fusion | flops 155648 | bytes 34880 | tf_op jit(solution)/shard_map/convert
  1.6 0.6 %pad_maximum_fusion.1.table_ref = bf16[64,256]{1,0:T(8,128)(2,1)} fusion(bf16[32,256]{1,0:T(8,128)(2,1)S(1)} %get-tuple-element.7, bf16[32,256]{1,0:T(8,128)(2,1)S(1)} %get-tuple-element.6), kind=kLoop, calls=%fused_computation.7 | loop fusion | flops 65536 | bytes 65536 | tf_op jit(solution)/shard_map/concatenate | solution.py:237
  2.3 40.6 %shard_map.50 = (f32[4,2,32,32]{3,2,1,0:T(8,128)}, bf16[4,2,3,32,1024]{4,3,2,1,0:T(8,128)(2,1)}) custom-call(bf16[3,2048,1024]{2,1,0:T(8,128)(2,1)} %bitcast.3, bf16[64,256]{1,0:T(8,128)(2,1)} %pad_maximum_fusion.1.table_ref, f32[1,1024]{1,0:T(1,128)} %bitcast.5), custom_call_target="tpu_custom_call" | custom-call | tf_op jit(solution)/shard_map/pallas_call | solution.py:244
  42.9 1.6 %copy.8 = f32[4,2,32,32]{3,2,1,0:T(8,128)} copy(f32[4,2,32,32]{3,2,1,0:T(8,128)} %get-tuple-element.12) | data formatting | bytes 65536
  44.4 2.7 %copy.9 = bf16[4,2,32,3,1024]{4,2,3,1,0:T(8,128)(2,1)} copy(bf16[4,2,32,3,1024]{4,2,3,1,0:T(8,128)(2,1)} %bitcast.4) | data formatting | bytes 3145728
  (5 shorter events, 0.1 us)

commit v3 on v2

--- a/solution.py
+++ b/solution.py
@@ -57,22 +57,25 @@
     return (new == old_new).astype(F32)
 
 
-def inverse_root(real, imag):
+def normalized(real, imag):
     norm = jnp.sqrt(
         jnp.sum(real * real + imag * imag, axis=(0, 1), keepdims=True)
     )
     upper = jnp.concatenate([real, -imag], axis=1)
     lower = jnp.concatenate([imag, real], axis=1)
-    y = jnp.concatenate([upper, lower], axis=0) / norm
+    return jnp.concatenate([upper, lower], axis=0) / norm
+
+
+def inverse_roots(ys):
     ident = eye(2 * NB)
-    z = None
+    zs = None
     for it in range(ITERS):
-        zy = y if z is None else dot_high(z, y)
-        s = 0.5 * (3.0 * ident - zy)
+        zys = ys if zs is None else [dot_high(z, y) for z, y in zip(zs, ys)]
+        steps = [0.5 * (3.0 * ident - zy) for zy in zys]
         if it < ITERS - 1:
-            y = dot_high(y, s)
-        z = s if z is None else dot_high(s, z)
-    return z
+            ys = [dot_high(y, s) for y, s in zip(ys, steps)]
+        zs = steps if zs is None else [dot_high(s, z) for s, z in zip(steps, zs)]
+    return zs
 
 
 def kernel(nt, ns, series, table_ref, w_ref, cross_ref, modes_ref,
@@ -111,6 +114,7 @@
             device_id={"tm": to}, device_id_type=MESH,
         )
 
+    order = gather_order(rows, lb, lf).astype(BF16)
     gram = jnp.zeros((rows, rows), F32)
 
     def consume(q, gram):
@@ -131,7 +135,10 @@
                 fixed = tail[per:] + halos[src][c * per:(c + 1) * per]
                 xall[c, src * part + main:(src + 1) * part, cols] = jnp.concatenate(
                     [tail[:per], fixed], axis=0).astype(BF16)
-            x = xall[c, :, cols]
+            x = jnp.dot(
+                order, xall[c, :, cols], preferred_element_type=F32
+            ).astype(BF16)
+            xall[c, :, cols] = x
             xw = x.astype(F32) * weight
             hi = xw.astype(BF16)
             lo = (xw - hi.astype(F32)).astype(BF16)
@@ -169,8 +176,6 @@
             gram = consume(q - 1, gram)
     gram = consume(nq - 1, gram)
 
-    order = gather_order(rows, lb, lf)
-    gram = dot_t(dot_high(order, gram), order, precision=lax.Precision.HIGHEST)
     parts = []
     for f in range(lf):
         a = f * 2 * NB
@@ -207,9 +212,10 @@
     for f in range(lf):
         cross_ref[f, 0] = total[2 * f]
         cross_ref[f, 1] = total[2 * f + 1]
+    zs = inverse_roots([normalized(total[2 * f], total[2 * f + 1]) for f in range(lf)])
     roots = []
     for f in range(lf):
-        z = inverse_root(total[2 * f], total[2 * f + 1]).astype(BF16).astype(F32)
+        z = zs[f].astype(BF16).astype(F32)
         pieces = []
         if f:
             pieces.append(jnp.zeros((2 * NB, f * 2 * NB), F32))
@@ -218,7 +224,6 @@
             pieces.append(jnp.zeros((2 * NB, (lf - 1 - f) * 2 * NB), F32))
         roots.append(jnp.concatenate(pieces, axis=1))
     mix = jnp.concatenate(roots, axis=0).astype(BF16)
-    mix = jnp.dot(mix, order.astype(BF16), preferred_element_type=F32).astype(BF16)
     for c in range(3):
         for q in range(nq):
             cols = pl.ds(q * CHUNK, CHUNK)

time: 47.4 us -> 44.2 us (0.932)
  Pallas kernels: 40.6 us -> 37.4 us
    pallas_call x1, Pallas kernels: 40.6 us -> 37.4 us  [on_device(): pl.pallas_call(functools.partial(kernel, nt, ns), out_shape=(jax.ShapeDty...]
where the time goes in v3:
time: 44.2 us; the launch traced here: 44 us
  Pallas kernels  37.4 us (85%)
  local copies, waits for them, and re-layouts  4.37 us (10%)
  other arithmetic  1.54 us (3%)
  between operations  0.67 us (2%)
    pallas_call x1, Pallas kernels, on_device(): pl.pallas_call(functools.partial(kernel, nt, ns), out_shape=(jax.ShapeDty...  37.4 us
    unnamed x2, local copies, waits for them, and re-layouts  4.31 us

profile of v3, /device:TPU:1, one launch (start us, length us, event | category | flops | bytes accessed | tf_op | source)
XLA Modules:
  0.0 44.0 jit_solution(17141420971097437759)
XLA Ops:
  0.7 0.9 %multiply_convert_fusion.1 = (bf16[16,1,512]{2,0,1:T(8,128)(2,1)S(1)}, bf16[16,1,512]{2,0,1:T(8,128)(2,1)S(1)}) fusion(f32[512]{0:T(512)S(1)} %subtract_multiply_fusion, s32[16]{0:T(128)} %param.5), kind=kLoop, calls=%fused_computation.9 | loop fusion | flops 155648 | bytes 34880 | tf_op jit(solution)/shard_map/convert
  1.6 0.6 %pad_maximum_fusion.1.table_ref = bf16[64,256]{1,0:T(8,128)(2,1)} fusion(bf16[32,256]{1,0:T(8,128)(2,1)S(1)} %get-tuple-element.7, bf16[32,256]{1,0:T(8,128)(2,1)S(1)} %get-tuple-element.6), kind=kLoop, calls=%fused_computation.7 | loop fusion | flops 65536 | bytes 65536 | tf_op jit(solution)/shard_map/concatenate | solution.py:242
  2.3 37.4 %shard_map.50 = (f32[4,2,32,32]{3,2,1,0:T(8,128)}, bf16[4,2,3,32,1024]{4,3,2,1,0:T(8,128)(2,1)}) custom-call(bf16[3,2048,1024]{2,1,0:T(8,128)(2,1)} %bitcast.3, bf16[64,256]{1,0:T(8,128)(2,1)} %pad_maximum_fusion.1.table_ref, f32[1,1024]{1,0:T(1,128)} %bitcast.5), custom_call_target="tpu_custom_call" | custom-call | tf_op jit(solution)/shard_map/pallas_call | solution.py:249
  39.7 1.6 %copy.8 = f32[4,2,32,32]{3,2,1,0:T(8,128)} copy(f32[4,2,32,32]{3,2,1,0:T(8,128)} %get-tuple-element.12) | data formatting | bytes 65536
  41.2 2.7 %copy.9 = bf16[4,2,32,3,1024]{4,2,3,1,0:T(8,128)(2,1)} copy(bf16[4,2,32,3,1024]{4,2,3,1,0:T(8,128)(2,1)} %bitcast.4) | data formatting | bytes 3145728
  (5 shorter events, 0.1 us)

commit v4 on v3

--- a/solution.py
+++ b/solution.py
@@ -78,9 +78,9 @@
     return zs
 
 
-def kernel(nt, ns, series, table_ref, w_ref, cross_ref, modes_ref,
+def kernel(nt, ns, series, table_ref, w_ref, total_ref, rows_ref,
            xbuf, send, land, xall, pair, ring, in_sem, a2a_send, a2a_recv,
-           core_send, core_recv, ar_send, ar_recv):
+           core_send, core_recv, ar_send, ar_recv, row_sem):
     t = lax.axis_index("tm")
     s = lax.axis_index("pts")
     nq = xbuf.shape[0]
@@ -116,6 +116,12 @@
 
     order = gather_order(rows, lb, lf).astype(BF16)
     gram = jnp.zeros((rows, rows), F32)
+
+    def row_copy(q):
+        cols = pl.ds(q * CHUNK, CHUNK)
+        return pltpu.make_async_copy(
+            xall.at[:, :, cols], rows_ref.at[:, :, cols], row_sem.at[q]
+        )
 
     def consume(q, gram):
         cols = pl.ds(q * CHUNK, CHUNK)
@@ -143,6 +149,7 @@
             hi = xw.astype(BF16)
             lo = (xw - hi.astype(F32)).astype(BF16)
             gram = gram + dot_t(hi, x) + dot_t(lo, x)
+        row_copy(q).start()
         return gram
 
     for q in range(nq):
@@ -208,33 +215,47 @@
     total = ring[chip]
     for k in range(1, nz):
         total = total + ring[lax.rem(chip - k + nz, nz)]
-    total = [total[:, k * NB:(k + 1) * NB] for k in range(2 * lf)]
-    for f in range(lf):
-        cross_ref[f, 0] = total[2 * f]
-        cross_ref[f, 1] = total[2 * f + 1]
-    zs = inverse_roots([normalized(total[2 * f], total[2 * f + 1]) for f in range(lf)])
-    roots = []
-    for f in range(lf):
-        z = zs[f].astype(BF16).astype(F32)
-        pieces = []
-        if f:
-            pieces.append(jnp.zeros((2 * NB, f * 2 * NB), F32))
-        pieces.append(z)
-        if f < lf - 1:
-            pieces.append(jnp.zeros((2 * NB, (lf - 1 - f) * 2 * NB), F32))
-        roots.append(jnp.concatenate(pieces, axis=1))
-    mix = jnp.concatenate(roots, axis=0).astype(BF16)
-    for c in range(3):
-        for q in range(nq):
-            cols = pl.ds(q * CHUNK, CHUNK)
-            out = jnp.dot(mix, xall[c, :, cols], preferred_element_type=F32)
-            modes_ref[:, :, c, :, cols] = out.astype(BF16).reshape(lf, 2, NB, CHUNK)
+    total_ref[...] = total
+    for q in range(nq):
+        row_copy(q).wait()
     for q in range(nq):
         for k in range(1, nt):
             peer_copy(q, k).wait_send()
     core_copy.wait_send()
     for k in range(1, nz):
         gram_copy(k).wait_send()
+
+
+def finish(total_ref, rows_ref, cross_ref, modes_ref, mix_ref):
+    lf = cross_ref.shape[0]
+
+    @pl.when(pl.program_id(0) == 0)
+    def _():
+        total = [total_ref[:, k * NB:(k + 1) * NB] for k in range(2 * lf)]
+        for f in range(lf):
+            cross_ref[f, 0] = total[2 * f]
+            cross_ref[f, 1] = total[2 * f + 1]
+        zs = inverse_roots(
+            [normalized(total[2 * f], total[2 * f + 1]) for f in range(lf)]
+        )
+        roots = []
+        for f in range(lf):
+            z = zs[f].astype(BF16).astype(F32)
+            pieces = []
+            if f:
+                pieces.append(jnp.zeros((2 * NB, f * 2 * NB), F32))
+            pieces.append(z)
+            if f < lf - 1:
+                pieces.append(jnp.zeros((2 * NB, (lf - 1 - f) * 2 * NB), F32))
+            roots.append(jnp.concatenate(pieces, axis=1))
+        mix_ref[...] = jnp.concatenate(roots, axis=0).astype(BF16)
+
+    for a in range(0, rows_ref.shape[2], CHUNK):
+        cols = pl.ds(a, CHUNK)
+        out = jnp.dot(
+            mix_ref[...], rows_ref[0, :, cols], preferred_element_type=F32
+        )
+        modes_ref[:, :, 0, :, cols] = out.astype(BF16).reshape(lf, 2, NB, CHUNK)
 
 
 def on_device(nt, ns, series, weights, freq_bins):
@@ -246,14 +267,14 @@
     rows = NB * 2 * lf
     part = lb * 2 * lf
     vmem = pl.BlockSpec(memory_space=pltpu.VMEM)
-    cross, modes = pl.pallas_call(
+    total, x = pl.pallas_call(
         functools.partial(kernel, nt, ns),
         out_shape=(
-            jax.ShapeDtypeStruct((lf, 2, NB, NB), F32),
-            jax.ShapeDtypeStruct((lf, 2, 3, NB, points), BF16),
+            jax.ShapeDtypeStruct((NB, 2 * lf * NB), F32),
+            jax.ShapeDtypeStruct((3, rows, points), BF16),
         ),
         in_specs=[pl.BlockSpec(memory_space=pl.ANY), vmem, vmem],
-        out_specs=(vmem, vmem),
+        out_specs=(vmem, pl.BlockSpec(memory_space=pl.ANY)),
         scratch_shapes=[
             pltpu.VMEM((nq, 3, series.shape[0], CHUNK), BF16),
             pltpu.VMEM((nq, nt, 3 * part + 8 * lf, CHUNK), BF16),
@@ -268,11 +289,30 @@
             pltpu.SemaphoreType.DMA,
             pltpu.SemaphoreType.DMA((ns // 2,)),
             pltpu.SemaphoreType.DMA((ns // 2,)),
+            pltpu.SemaphoreType.DMA((nq,)),
         ],
         compiler_params=pltpu.CompilerParams(
             collective_id=0, has_side_effects=True, vmem_limit_bytes=56 * 2**20
         ),
     )(series.transpose(1, 0, 2), table, weights.reshape(1, points))
+    cross, modes = pl.pallas_call(
+        finish,
+        grid=(3,),
+        out_shape=(
+            jax.ShapeDtypeStruct((lf, 2, NB, NB), F32),
+            jax.ShapeDtypeStruct((lf, 2, 3, NB, points), BF16),
+        ),
+        in_specs=[
+            pl.BlockSpec((NB, 2 * lf * NB), lambda c: (0, 0)),
+            pl.BlockSpec((1, rows, points), lambda c: (c, 0, 0)),
+        ],
+        out_specs=(
+            pl.BlockSpec((lf, 2, NB, NB), lambda c: (0, 0, 0, 0)),
+            pl.BlockSpec((lf, 2, 1, NB, points), lambda c: (0, 0, c, 0, 0)),
+        ),
+        scratch_shapes=[pltpu.VMEM((rows, rows), BF16)],
+        compiler_params=pltpu.CompilerParams(vmem_limit_bytes=56 * 2**20),
+    )(total, x)
     return cross, modes.transpose(0, 1, 3, 2, 4)
 
 

time: 44.2 us -> 42.6 us (0.964)
  local copies, waits for them, and re-layouts: 4.37 us -> 0.06 us
  Pallas kernels: 37.4 us -> 40.1 us
    pallas_call x0 -> x1, Pallas kernels: none -> 5.75 us  [on_device(): pl.pallas_call(finish, grid=(3,), out_shape=(jax.ShapeDtypeStruct((lf, 2,...]
    unnamed x2 -> x0, local copies, waits for them, and re-layouts: 4.31 us -> none
    pallas_call x1, Pallas kernels: 37.4 us -> 34.3 us  [on_device(): pl.pallas_call(functools.partial(kernel, nt, ns), out_shape=(jax.ShapeDty...]
where the time goes in v4:
time: 42.6 us; the launch traced here: 42.3 us
  Pallas kernels  40.1 us (94%)
  other arithmetic  1.54 us (4%)
  between operations  0.67 us (2%)
    pallas_call x1, Pallas kernels, on_device(): pl.pallas_call(functools.partial(kernel, nt, ns), out_shape=(jax.ShapeDty...  34.3 us
    pallas_call x1, Pallas kernels, on_device(): pl.pallas_call(finish, grid=(3,), out_shape=(jax.ShapeDtypeStruct((lf, 2,...  5.75 us
    another operation x1, other arithmetic  0.87 us

profile of v4, /device:TPU:1, one launch (start us, length us, event | category | flops | bytes accessed | tf_op | source)
XLA Modules:
  0.0 42.3 jit_solution(12788894372205643937)
XLA Ops:
  0.7 0.9 %multiply_convert_fusion.1 = (bf16[16,1,512]{2,0,1:T(8,128)(2,1)S(1)}, bf16[16,1,512]{2,0,1:T(8,128)(2,1)S(1)}) fusion(f32[512]{0:T(512)S(1)} %subtract_multiply_fusion, s32[16]{0:T(128)} %param.5), kind=kLoop, calls=%fused_computation.9 | loop fusion | flops 155648 | bytes 34880 | tf_op jit(solution)/shard_map/convert
  1.6 0.6 %pad_maximum_fusion.1.table_ref = bf16[64,256]{1,0:T(8,128)(2,1)} fusion(bf16[32,256]{1,0:T(8,128)(2,1)S(1)} %get-tuple-element.11, bf16[32,256]{1,0:T(8,128)(2,1)S(1)} %get-tuple-element.10), kind=kLoop, calls=%fused_computation.7 | loop fusion | flops 65536 | bytes 65536 | tf_op jit(solution)/shard_map/concatenate | solution.py:263
  2.3 34.3 %shard_map.50 = (f32[32,256]{1,0:T(8,128)}, bf16[3,256,1024]{2,1,0:T(8,128)(2,1)}) custom-call(bf16[3,2048,1024]{2,1,0:T(8,128)(2,1)} %bitcast.3, bf16[64,256]{1,0:T(8,128)(2,1)} %pad_maximum_fusion.1.table_ref, f32[1,1024]{1,0:T(1,128)} %bitcast.4), custom_call_target="tpu_custom_call" | custom-call | tf_op jit(solution)/shard_map/pallas_call | solution.py:270
  36.6 5.7 %shard_map.51 = (f32[4,2,32,32]{3,2,1,0:T(8,128)}, bf16[4,2,3,32,1024]{4,3,2,1,0:T(8,128)(2,1)}) custom-call(f32[32,256]{1,0:T(8,128)} %get-tuple-element.6.total_ref, bf16[3,256,1024]{2,1,0:T(8,128)(2,1)} %get-tuple-element.7.rows_ref), custom_call_target="tpu_custom_call" | custom-call | tf_op jit(solution)/shard_map/pallas_call | solution.py:298
  (5 shorter events, 0.1 us)

commit v5 on v4

--- a/solution.py
+++ b/solution.py
@@ -89,10 +89,14 @@
     per = 2 * lf
     part = lb * per
     rows = nt * part
-    for q in range(nq):
-        pltpu.make_async_copy(
+    peers = sorted(range(1, nt), key=lambda k: abs(2 * k - nt))
+
+    def load(q):
+        return pltpu.make_async_copy(
             series.at[:, :, pl.ds(q * CHUNK, CHUNK)], xbuf.at[q], in_sem.at[q]
-        ).start()
+        )
+
+    load(0).start()
     barrier = pltpu.get_barrier_semaphore()
     for k in range(1, nt):
         pl.semaphore_signal(barrier, inc=1, device_id={"tm": lax.rem(t + k, nt)},
@@ -106,11 +110,12 @@
                             device_id_type=MESH)
     pl.semaphore_wait(barrier, nt - 1 + nz)
 
-    def peer_copy(q, k):
+    def peer_copy(q, k, c):
         to = lax.rem(t + k, nt)
+        sent = pl.ds(c * part, part if c < 2 else part + 4 * per)
         return pltpu.make_async_remote_copy(
-            src_ref=send.at[q, to], dst_ref=land.at[q, k],
-            send_sem=a2a_send.at[q, k], recv_sem=a2a_recv.at[q, k],
+            src_ref=send.at[q, to, sent], dst_ref=land.at[q, k, sent],
+            send_sem=a2a_send.at[q, k, c], recv_sem=a2a_recv.at[q, k, c],
             device_id={"tm": to}, device_id_type=MESH,
         )
 
@@ -126,7 +131,8 @@
     def consume(q, gram):
         cols = pl.ds(q * CHUNK, CHUNK)
         for k in range(1, nt):
-            peer_copy(q, k).wait_recv()
+            for c in range(3):
+                peer_copy(q, k, c).wait_recv()
         weight = w_ref[:, q * CHUNK:(q + 1) * CHUNK]
         halos = [
             land[q, lax.rem(t - src - 1 + nt, nt), 3 * part:, :].astype(F32)
@@ -153,9 +159,9 @@
         return gram
 
     for q in range(nq):
-        pltpu.make_async_copy(
-            series.at[:, :, pl.ds(q * CHUNK, CHUNK)], xbuf.at[q], in_sem.at[q]
-        ).wait()
+        load(q).wait()
+        if q + 1 < nq:
+            load(q + 1).start()
         edges = []
         for c in range(3):
             firsts, seconds = [], []
@@ -171,13 +177,14 @@
                 send[q, d, c * part:(c + 1) * part, :] = jnp.concatenate(
                     [v[d * per:(d + 1) * per] for v in sums], axis=0
                 ).astype(BF16)
-        edges.append(jnp.zeros((2 * NF, CHUNK), F32))
-        for d in range(nt):
-            send[q, d, 3 * part:, :] = jnp.concatenate(
-                [v[d * per:(d + 1) * per] for v in edges], axis=0
-            ).astype(BF16)
-        for k in range(1, nt):
-            peer_copy(q, k).start()
+            if c == 2:
+                edges.append(jnp.zeros((2 * NF, CHUNK), F32))
+                for d in range(nt):
+                    send[q, d, 3 * part:, :] = jnp.concatenate(
+                        [v[d * per:(d + 1) * per] for v in edges], axis=0
+                    ).astype(BF16)
+            for k in peers:
+                peer_copy(q, k, c).start()
         land[q, 0] = send[q, t]
         if q > 0:
             gram = consume(q - 1, gram)
@@ -220,7 +227,8 @@
         row_copy(q).wait()
     for q in range(nq):
         for k in range(1, nt):
-            peer_copy(q, k).wait_send()
+            for c in range(3):
+                peer_copy(q, k, c).wait_send()
     core_copy.wait_send()
     for k in range(1, nz):
         gram_copy(k).wait_send()
@@ -283,8 +291,8 @@
             pltpu.VMEM((2, NB, 2 * lf * NB), F32),
             pltpu.VMEM((ns // 2, NB, 2 * lf * NB), F32),
             pltpu.SemaphoreType.DMA((nq,)),
-            pltpu.SemaphoreType.DMA((nq, nt)),
-            pltpu.SemaphoreType.DMA((nq, nt)),
+            pltpu.SemaphoreType.DMA((nq, nt, 3)),
+            pltpu.SemaphoreType.DMA((nq, nt, 3)),
             pltpu.SemaphoreType.DMA,
             pltpu.SemaphoreType.DMA,
             pltpu.SemaphoreType.DMA((ns // 2,)),

time: 42.6 us -> 43.3 us (1.016)
  Pallas kernels: 40.1 us -> 40.8 us
    pallas_call x1, Pallas kernels: 34.3 us -> 35 us  [on_device(): pl.pallas_call(functools.partial(kernel, nt, ns), out_shape=(jax.ShapeDty...]
where the time goes in v5:
time: 43.3 us; the launch traced here: 43 us
  Pallas kernels  40.8 us (94%)
  other arithmetic  1.54 us (4%)
  between operations  0.67 us (2%)
    pallas_call x1, Pallas kernels, on_device(): pl.pallas_call(functools.partial(kernel, nt, ns), out_shape=(jax.ShapeDty...  35 us
    pallas_call x1, Pallas kernels, on_device(): pl.pallas_call(finish, grid=(3,), out_shape=(jax.ShapeDtypeStruct((lf, 2,...  5.75 us
    another operation x1, other arithmetic  0.87 us

profile of v5, /device:TPU:1, one launch (start us, length us, event | category | flops | bytes accessed | tf_op | source)
XLA Modules:
  0.0 43.0 jit_solution(4452067729215058017)
XLA Ops:
  0.7 0.9 %multiply_convert_fusion.1 = (bf16[16,1,512]{2,0,1:T(8,128)(2,1)S(1)}, bf16[16,1,512]{2,0,1:T(8,128)(2,1)S(1)}) fusion(f32[512]{0:T(512)S(1)} %subtract_multiply_fusion, s32[16]{0:T(128)} %param.5), kind=kLoop, calls=%fused_computation.9 | loop fusion | flops 155648 | bytes 34880 | tf_op jit(solution)/shard_map/convert
  1.6 0.6 %pad_maximum_fusion.1.table_ref = bf16[64,256]{1,0:T(8,128)(2,1)} fusion(bf16[32,256]{1,0:T(8,128)(2,1)S(1)} %get-tuple-element.11, bf16[32,256]{1,0:T(8,128)(2,1)S(1)} %get-tuple-element.10), kind=kLoop, calls=%fused_computation.7 | loop fusion | flops 65536 | bytes 65536 | tf_op jit(solution)/shard_map/concatenate | solution.py:271
  2.3 35.0 %shard_map.50 = (f32[32,256]{1,0:T(8,128)}, bf16[3,256,1024]{2,1,0:T(8,128)(2,1)}) custom-call(bf16[3,2048,1024]{2,1,0:T(8,128)(2,1)} %bitcast.3, bf16[64,256]{1,0:T(8,128)(2,1)} %pad_maximum_fusion.1.table_ref, f32[1,1024]{1,0:T(1,128)} %bitcast.4), custom_call_target="tpu_custom_call" | custom-call | tf_op jit(solution)/shard_map/pallas_call | solution.py:278
  37.3 5.8 %shard_map.51 = (f32[4,2,32,32]{3,2,1,0:T(8,128)}, bf16[4,2,3,32,1024]{4,3,2,1,0:T(8,128)(2,1)}) custom-call(f32[32,256]{1,0:T(8,128)} %get-tuple-element.6.total_ref, bf16[3,256,1024]{2,1,0:T(8,128)(2,1)} %get-tuple-element.7.rows_ref), custom_call_target="tpu_custom_call" | custom-call | tf_op jit(solution)/shard_map/pallas_call | solution.py:306
  (5 shorter events, 0.1 us)

commit v6 on v4

--- a/solution.py
+++ b/solution.py
@@ -83,7 +83,13 @@
            core_send, core_recv, ar_send, ar_recv, row_sem):
     t = lax.axis_index("tm")
     s = lax.axis_index("pts")
-    nq = xbuf.shape[0]
+    points = xbuf.shape[2]
+    cuts = [0, *range(CHUNK // 2, points, CHUNK), points]
+    nq = len(cuts) - 1
+
+    def span(q):
+        return pl.ds(cuts[q], cuts[q + 1] - cuts[q])
+
     lb = NB // nt
     lf = NF // nt
     per = 2 * lf
@@ -91,7 +97,7 @@
     rows = nt * part
     for q in range(nq):
         pltpu.make_async_copy(
-            series.at[:, :, pl.ds(q * CHUNK, CHUNK)], xbuf.at[q], in_sem.at[q]
+            series.at[:, :, span(q)], xbuf.at[:, :, span(q)], in_sem.at[q]
         ).start()
     barrier = pltpu.get_barrier_semaphore()
     for k in range(1, nt):
@@ -109,7 +115,7 @@
     def peer_copy(q, k):
         to = lax.rem(t + k, nt)
         return pltpu.make_async_remote_copy(
-            src_ref=send.at[q, to], dst_ref=land.at[q, k],
+            src_ref=send.at[to, :, span(q)], dst_ref=land.at[k, :, span(q)],
             send_sem=a2a_send.at[q, k], recv_sem=a2a_recv.at[q, k],
             device_id={"tm": to}, device_id_type=MESH,
         )
@@ -118,26 +124,26 @@
     gram = jnp.zeros((rows, rows), F32)
 
     def row_copy(q):
-        cols = pl.ds(q * CHUNK, CHUNK)
+        cols = span(q)
         return pltpu.make_async_copy(
             xall.at[:, :, cols], rows_ref.at[:, :, cols], row_sem.at[q]
         )
 
     def consume(q, gram):
-        cols = pl.ds(q * CHUNK, CHUNK)
+        cols = span(q)
         for k in range(1, nt):
             peer_copy(q, k).wait_recv()
-        weight = w_ref[:, q * CHUNK:(q + 1) * CHUNK]
+        weight = w_ref[:, cols]
         halos = [
-            land[q, lax.rem(t - src - 1 + nt, nt), 3 * part:, :].astype(F32)
+            land[lax.rem(t - src - 1 + nt, nt), 3 * part:, cols].astype(F32)
             for src in range(nt)
         ]
         for c in range(3):
             for src in range(nt):
                 at = lax.rem(t - src + nt, nt)
                 main = part - 2 * per
-                xall[c, src * part:src * part + main, cols] = land[q, at, c * part:c * part + main, :]
-                tail = land[q, at, c * part + main:(c + 1) * part, :].astype(F32)
+                xall[c, src * part:src * part + main, cols] = land[at, c * part:c * part + main, cols]
+                tail = land[at, c * part + main:(c + 1) * part, cols].astype(F32)
                 fixed = tail[per:] + halos[src][c * per:(c + 1) * per]
                 xall[c, src * part + main:(src + 1) * part, cols] = jnp.concatenate(
                     [tail[:per], fixed], axis=0).astype(BF16)
@@ -154,13 +160,13 @@
 
     for q in range(nq):
         pltpu.make_async_copy(
-            series.at[:, :, pl.ds(q * CHUNK, CHUNK)], xbuf.at[q], in_sem.at[q]
+            series.at[:, :, span(q)], xbuf.at[:, :, span(q)], in_sem.at[q]
         ).wait()
         edges = []
         for c in range(3):
             firsts, seconds = [], []
             for j in range(lb):
-                block = xbuf[q, c, j * HALF:(j + 1) * HALF, :]
+                block = xbuf[c, j * HALF:(j + 1) * HALF, span(q)]
                 both = jnp.dot(table_ref[...], block, preferred_element_type=F32)
                 firsts.append(both[:2 * NF])
                 seconds.append(both[2 * NF:])
@@ -168,17 +174,17 @@
             sums.append(firsts[lb - 1])
             edges.append(seconds[0])
             for d in range(nt):
-                send[q, d, c * part:(c + 1) * part, :] = jnp.concatenate(
+                send[d, c * part:(c + 1) * part, span(q)] = jnp.concatenate(
                     [v[d * per:(d + 1) * per] for v in sums], axis=0
                 ).astype(BF16)
-        edges.append(jnp.zeros((2 * NF, CHUNK), F32))
+        edges.append(jnp.zeros(edges[0].shape, F32))
         for d in range(nt):
-            send[q, d, 3 * part:, :] = jnp.concatenate(
+            send[d, 3 * part:, span(q)] = jnp.concatenate(
                 [v[d * per:(d + 1) * per] for v in edges], axis=0
             ).astype(BF16)
         for k in range(1, nt):
             peer_copy(q, k).start()
-        land[q, 0] = send[q, t]
+        land[0, :, span(q)] = send[t, :, span(q)]
         if q > 0:
             gram = consume(q - 1, gram)
     gram = consume(nq - 1, gram)
@@ -262,7 +268,7 @@
     table = build_table(freq_bins)
     table = jnp.concatenate([table[:, :HALF], table[:, HALF:]], axis=0)
     points = series.shape[2]
-    nq = points // CHUNK
+    nq = points // CHUNK + 1
     lb, lf = NB // nt, NF // nt
     rows = NB * 2 * lf
     part = lb * 2 * lf
@@ -276,9 +282,9 @@
         in_specs=[pl.BlockSpec(memory_space=pl.ANY), vmem, vmem],
         out_specs=(vmem, pl.BlockSpec(memory_space=pl.ANY)),
         scratch_shapes=[
-            pltpu.VMEM((nq, 3, series.shape[0], CHUNK), BF16),
-            pltpu.VMEM((nq, nt, 3 * part + 8 * lf, CHUNK), BF16),
-            pltpu.VMEM((nq, nt, 3 * part + 8 * lf, CHUNK), BF16),
+            pltpu.VMEM((3, series.shape[0], points), BF16),
+            pltpu.VMEM((nt, 3 * part + 8 * lf, points), BF16),
+            pltpu.VMEM((nt, 3 * part + 8 * lf, points), BF16),
             pltpu.VMEM((3, rows, points), BF16),
             pltpu.VMEM((2, NB, 2 * lf * NB), F32),
             pltpu.VMEM((ns // 2, NB, 2 * lf * NB), F32),

time: 42.6 us -> 42.4 us (level)
  no operation moved by 1% of the time
where the time goes in v6:
time: 42.4 us; the launch traced here: 42.1 us
  Pallas kernels  39.9 us (94%)
  other arithmetic  1.54 us (4%)
  between operations  0.67 us (2%)
    pallas_call x1, Pallas kernels, on_device(): pl.pallas_call(functools.partial(kernel, nt, ns), out_shape=(jax.ShapeDty...  34.1 us
    pallas_call x1, Pallas kernels, on_device(): pl.pallas_call(finish, grid=(3,), out_shape=(jax.ShapeDtypeStruct((lf, 2,...  5.75 us
    another operation x1, other arithmetic  0.87 us

profile of v6, /device:TPU:1, one launch (start us, length us, event | category | flops | bytes accessed | tf_op | source)
XLA Modules:
  0.0 42.1 jit_solution(6236949734952238375)
XLA Ops:
  0.7 0.9 %multiply_convert_fusion.1 = (bf16[16,1,512]{2,0,1:T(8,128)(2,1)S(1)}, bf16[16,1,512]{2,0,1:T(8,128)(2,1)S(1)}) fusion(f32[512]{0:T(512)S(1)} %subtract_multiply_fusion, s32[16]{0:T(128)} %param.5), kind=kLoop, calls=%fused_computation.9 | loop fusion | flops 155648 | bytes 34880 | tf_op jit(solution)/shard_map/convert
  1.6 0.6 %pad_maximum_fusion.1.table_ref = bf16[64,256]{1,0:T(8,128)(2,1)} fusion(bf16[32,256]{1,0:T(8,128)(2,1)S(1)} %get-tuple-element.11, bf16[32,256]{1,0:T(8,128)(2,1)S(1)} %get-tuple-element.10), kind=kLoop, calls=%fused_computation.7 | loop fusion | flops 65536 | bytes 65536 | tf_op jit(solution)/shard_map/concatenate | solution.py:269
  2.3 34.1 %shard_map.50 = (f32[32,256]{1,0:T(8,128)}, bf16[3,256,1024]{2,1,0:T(8,128)(2,1)}) custom-call(bf16[3,2048,1024]{2,1,0:T(8,128)(2,1)} %bitcast.3, bf16[64,256]{1,0:T(8,128)(2,1)} %pad_maximum_fusion.1.table_ref, f32[1,1024]{1,0:T(1,128)} %bitcast.4), custom_call_target="tpu_custom_call" | custom-call | tf_op jit(solution)/shard_map/pallas_call | solution.py:276
  36.4 5.8 %shard_map.51 = (f32[4,2,32,32]{3,2,1,0:T(8,128)}, bf16[4,2,3,32,1024]{4,3,2,1,0:T(8,128)(2,1)}) custom-call(f32[32,256]{1,0:T(8,128)} %get-tuple-element.6.total_ref, bf16[3,256,1024]{2,1,0:T(8,128)(2,1)} %get-tuple-element.7.rows_ref), custom_call_target="tpu_custom_call" | custom-call | tf_op jit(solution)/shard_map/pallas_call | solution.py:304
  (5 shorter events, 0.1 us)
